TPU v7x, 32 devices: a whole 2x2x4 slice. The times are simulated.
32 devices in a mesh: expert: 4 (over y, x), replica: 8 (over z, core).
Axes of the slice: x: 2, y: 2, z: 4, core: 2. Of those that a mesh axis runs over, the one named last changes fastest.
Arguments:
- tokens: bfloat16 [4096, 2560], P(('expert', 'replica')), may hold values from -6 to 6
- cotangent: bfloat16 [4096, 2560], P(('expert', 'replica')), may hold values from -4 to 4
- partner: int32 [4096, 1], P(('expert', 'replica')), may hold values from 0 to 3; in each aligned block of 128 rows (0 to 127, 128 to 255, ...) at most 40 rows name the same one
- combine: int32 [4096, 2], P(('expert', 'replica')), may hold values from 1 to 8
- counts: int32 [32], P(('expert', 'replica')), may hold values from 32 to 128, as said below
- w_gate: bfloat16 [4, 2560, 768], P('expert', 'replica'), may hold values from -0.125 to 0.125
- w_up: bfloat16 [4, 2560, 768], P('expert', 'replica'), may hold values from -0.125 to 0.125
- w_down: bfloat16 [4, 768, 2560], P('expert', 'replica'), may hold values from -0.21875 to 0.21875
Outputs:
- token_grad: bfloat16 [4096, 2560], P(('expert', 'replica'))
- grad_down: bfloat16 [4, 768, 2560], P('expert', 'replica')
Inputs may be any that keep to these rules, and one draw needn't show every extreme that they name: `partner`: within the 128 rows of one device no expert index is named by more than 40 rows, and some device names one exactly 40 times. `counts`: some device has all 128 slots real.
All inputs are finite; a program needn't handle non-finite values.
Results may differ from a plain program's by a relative error of at most 0.017.
Values may be sent and summed in bfloat16 or wider, within the bound.
A program may use at most 64 MiB of HBM per device.

v0:
```python
import jax
import jax.numpy as jnp
from jax import lax
from jax.sharding import PartitionSpec as P


def against_rows(left, matrix):
    return lax.dot_general(
        left, matrix, (((1,), (1,)), ((), ())), preferred_element_type=jnp.float32
    )


def expert_backward(inputs, upstream, gate_w, up_w, down_w):
    gate_act = jnp.dot(inputs, gate_w, preferred_element_type=jnp.float32)
    up_act = jnp.dot(inputs, up_w, preferred_element_type=jnp.float32)
    sigmoid_gate = jax.nn.sigmoid(gate_act)
    swish_gate = gate_act * sigmoid_gate
    hidden = (swish_gate * up_act).astype(jnp.bfloat16)
    hidden_grad = against_rows(upstream, down_w)
    gate_grad = (
        hidden_grad * up_act * sigmoid_gate * (1.0 + gate_act * (1.0 - sigmoid_gate))
    ).astype(jnp.bfloat16)
    up_grad = (hidden_grad * swish_gate).astype(jnp.bfloat16)
    input_grad = against_rows(gate_grad, gate_w) + against_rows(up_grad, up_w)
    return (hidden, input_grad)


def local(tokens, cotangent, partner, combine, counts, w_gate, w_up, w_down):
    tok_rows = tokens.shape[0]
    width = tokens.shape[1]
    expert_count = lax.axis_size("expert")
    capacity = max(2, (5 * tok_rows // 4 + expert_count - 1) // expert_count)
    positions = jnp.arange(tok_rows, dtype=jnp.int32)
    valid_rows = positions < counts[0]
    weights = combine.astype(jnp.float32)
    weight_sum = weights[:, 0] + weights[:, 1]
    share_home = jnp.where(valid_rows, weights[:, 0] / weight_sum, 0.0)
    share_away = jnp.where(valid_rows, weights[:, 1] / weight_sum, 0.0)
    upstream = cotangent.astype(jnp.float32)
    q_home = (upstream * share_home[:, None]).astype(jnp.bfloat16)
    q_away = (upstream * share_away[:, None]).astype(jnp.bfloat16)
    gate_full, up_full, down_full = (
        lax.all_gather(w_gate, "replica", axis=1, tiled=True),
        lax.all_gather(w_up, "replica", axis=1, tiled=True),
        lax.all_gather(w_down, "replica", axis=1, tiled=True),
    )
    gate_w = gate_full.reshape(gate_full.shape[1], gate_full.shape[2])
    up_w = up_full.reshape(up_full.shape[1], up_full.shape[2])
    down_w = down_full.reshape(down_full.shape[1], down_full.shape[2])
    target = partner[:, 0]
    onehot_rows = (target[:, None] == jnp.arange(expert_count, dtype=jnp.int32)[None, :]).astype(
        jnp.int32
    )
    rank_within = jnp.sum((jnp.cumsum(onehot_rows, axis=0) - onehot_rows) * onehot_rows, axis=1)
    destination = target * capacity + rank_within
    placing = (
        jnp.arange(expert_count * capacity, dtype=jnp.int32)[:, None] == destination[None, :]
    ).astype(jnp.bfloat16)
    send_x = (
        jnp.dot(placing, tokens, preferred_element_type=jnp.float32)
        .astype(jnp.bfloat16)
        .reshape(expert_count, capacity, width)
    )
    send_q = (
        jnp.dot(placing, q_away, preferred_element_type=jnp.float32)
        .astype(jnp.bfloat16)
        .reshape(expert_count, capacity, width)
    )
    hidden_home, grad_home = expert_backward(tokens, q_home, gate_w, up_w, down_w)
    x_there = lax.all_to_all(send_x, "expert", split_axis=0, concat_axis=0, tiled=True)
    q_there = lax.all_to_all(send_q, "expert", split_axis=0, concat_axis=0, tiled=True)
    item_count = x_there.shape[1]
    hidden_there, grad_there = expert_backward(
        x_there.reshape(-1, width), q_there.reshape(-1, width), gate_w, up_w, down_w
    )
    returned = lax.all_to_all(
        grad_there.astype(jnp.bfloat16).reshape(expert_count, item_count, width),
        "expert",
        split_axis=0,
        concat_axis=0,
        tiled=True,
    )
    returned, hidden_away, q_there = (
        returned,
        hidden_there.reshape(expert_count, item_count, -1),
        q_there,
    )
    contract = (((0,), (0,)), ((), ()))
    flat_returned = returned.reshape(expert_count * capacity, width)
    grad_away = lax.dot_general(
        placing, flat_returned, contract, preferred_element_type=jnp.float32
    )
    token_grad = (grad_home + grad_away).astype(jnp.bfloat16)
    flat_hidden = hidden_away.reshape(expert_count * capacity, -1)
    flat_q = q_there.reshape(expert_count * capacity, width)
    grad_down = lax.psum_scatter(
        (
            lax.dot_general(hidden_home, q_home, contract, preferred_element_type=jnp.float32)
            + lax.dot_general(flat_hidden, flat_q, contract, preferred_element_type=jnp.float32)
        ).astype(jnp.bfloat16),
        "replica",
        scatter_dimension=0,
        tiled=True,
    )
    return (token_grad, grad_down[None])


def solution(mesh):
    placed = (
        P(("expert", "replica"), None),
        P(("expert", "replica"), None),
        P(("expert", "replica"), None),
        P(("expert", "replica"), None),
        P(("expert", "replica")),
        P("expert", "replica", None),
        P("expert", "replica", None),
        P("expert", "replica", None),
    )
    return jax.shard_map(
        local,
        mesh=mesh,
        in_specs=placed,
        out_specs=(P(("expert", "replica"), None), P("expert", "replica", None)),
        check_vma=False,
    )
```

profile of v0, /device:TPU:0, one launch (start us, length us, event | category | flops | bytes accessed | tf_op | source)
XLA Modules:
  0.0 203.4 jit_solution(1149341398967520120)
XLA Ops:
  9.4 0.7 fusion.45
  10.3 0.8 select_reduce_fusion
  11.8 1.2 convolution_convert_fusion
  13.1 5.2 %all-to-all-start.1 = ((bf16[4,40,2560]{2,1,0:T(8,128)(2,1)}), bf16[4,40,2560]{2,1,0:T(8,128)(2,1)S(1)}, u32[]{:S(2)}, u32[]{:S(2)}) async-start(bf16[4,40,2560]{2,1,0:T(8,128)(2,1)} %bitcast.9), calls=%async_computation.1 | async-start | bytes 1638400 | tf_op jit(solution)/shard_map/all_to_all | solution.py:70
  19.0 1.3 convolution_convert_fusion.1
  20.3 36.9 %all-gather.8.cloned.1.call-done = bf16[1,2560,768]{2,1,0:T(8,128)(2,1)} async-done(((bf16[1,320,768]{2,1,0:T(8,128)(2,1)}), bf16[1,2560,768]{2,1,0:T(8,128)(2,1)}) %all-gather.8.cloned.1.call-update) | async-done | bytes 3932176 | tf_op jit(solution)/shard_map/all_gather | solution.py:43
  57.2 2.8 %fusion.6 = f32[128,768]{1,0:T(8,128)S(1)} fusion(bf16[128,2560]{1,0:T(8,128)(2,1)S(1)} %copy-done, bf16[1,2560,768]{2,1,0:T(8,128)(2,1)} %all-gather.8.cloned.1.call-done), kind=kOutput, calls=%fused_computation.7 | convolution fusion | flops 503316480 | bytes 4980736 | tf_op jit(solution)/shard_map/dot_general | solution.py:14
  60.0 3.7 %all-to-all-start = ((bf16[4,40,2560]{2,1,0:T(8,128)(2,1)}), bf16[4,40,2560]{2,1,0:T(8,128)(2,1)S(1)}, u32[]{:S(2)}, u32[]{:S(2)}) async-start(bf16[4,40,2560]{2,1,0:T(8,128)(2,1)} %bitcast.56), calls=%async_computation | async-start | bytes 1638400 | tf_op jit(solution)/shard_map/all_to_all | solution.py:71
  63.6 3.2 %fusion.2 = f32[160,768]{1,0:T(8,128)S(1)} fusion(bf16[160,2560]{1,0:T(8,128)(2,1)S(1)} %bitcast.52, bf16[1,2560,768]{2,1,0:T(8,128)(2,1)} %all-gather.8.cloned.1.call-done), kind=kOutput, calls=%fused_computation.3 | convolution fusion | flops 629145600 | bytes 5242880 | tf_op jit(solution)/shard_map/dot_general | solution.py:14
  66.8 35.6 %all-gather.6.cloned.1.call-done = bf16[1,2560,768]{2,1,0:T(8,128)(2,1)} async-done(((bf16[1,320,768]{2,1,0:T(8,128)(2,1)}), bf16[1,2560,768]{2,1,0:T(8,128)(2,1)}) %all-gather.6.cloned.1.call-update) | async-done | bytes 3932176 | tf_op jit(solution)/shard_map/all_gather | solution.py:44
  102.5 3.8 %fusion.10 = f32[160,768]{1,0:T(8,128)} fusion(bf16[160,2560]{1,0:T(8,128)(2,1)S(1)} %bitcast.53, bf16[1,2560,768]{2,1,0:T(8,128)(2,1)} %all-gather.6.cloned.1.call-done), kind=kOutput, calls=%fused_computation.11 | convolution fusion | flops 629145600 | bytes 5242880 | tf_op jit(solution)/shard_map/dot_general | solution.py:15
  107.7 4.5 %fusion.36 = f32[768,2560]{1,0:T(8,128)} fusion(bf16[128,2560]{1,0:T(8,128)(2,1)S(1)} %copy-done.7, f32[128]{0:T(128)S(1)} %get-tuple-element.3, f32[128,768]{1,0:T(8,128)S(1)} %fusion.14, f32[128,768]{1,0:T(8,128)S(1)} %fusion.6), kind=kOutput, calls=%fused_computation.43 | convolution fusion | flops 504889344 | bytes 9306624 | tf_op jit(solution)/shard_map/dot_general | solution.py:98
  112.2 6.4 %add_convert_fusion = bf16[768,2560]{1,0:T(8,128)(2,1)} fusion(f32[768,2560]{1,0:T(8,128)} %fusion.36, bf16[160,2560]{1,0:T(8,128)(2,1)S(1)} %bitcast.54, f32[160,768]{1,0:T(8,128)S(1)} %copy-done.9, f32[160,768]{1,0:T(8,128)S(1)} %fusion.2), kind=kOutput, calls=%fused_computation | convolution fusion | flops 633815040 | bytes 13598720 | tf_op jit(solution)/shard_map/dot_general | solution.py:99
  118.7 29.1 %all-gather.4.cloned.1.call-done = bf16[1,768,2560]{2,1,0:T(8,128)(2,1)} async-done(((bf16[1,96,2560]{2,1,0:T(8,128)(2,1)}), bf16[1,768,2560]{2,1,0:T(8,128)(2,1)}) %all-gather.4.cloned.1.call-update) | async-done | bytes 3932176 | tf_op jit(solution)/shard_map/all_gather | solution.py:45
  147.7 3.7 %fusion.16 = f32[160,768]{1,0:T(8,128)S(1)} fusion(bf16[160,2560]{1,0:T(8,128)(2,1)S(1)} %bitcast.55, bf16[1,768,2560]{2,1,0:T(8,128)(2,1)} %all-gather.4.cloned.1.call-done), kind=kOutput, calls=%fused_computation.17 | convolution fusion | flops 629145600 | bytes 5242880 | tf_op jit(solution)/shard_map/dot_general | solution.py:8
  151.4 1.4 fusion
  153.6 2.4 %fusion.26 = bf16[160,2560]{1,0:T(8,128)(2,1)} fusion(f32[160,2560]{1,0:T(8,128)S(1)} %fusion, bf16[1,2560,768]{2,1,0:T(8,128)(2,1)S(1)} %copy-done.2, f32[160,768]{1,0:T(8,128)S(1)} %fusion.16, f32[160,768]{1,0:T(8,128)S(1)} %fusion.2), kind=kOutput, calls=%fused_computation.24 | convolution fusion | flops 630702080 | bytes 7372800 | tf_op jit(solution)/shard_map/dot_general | solution.py:8
  155.9 4.3 %all-to-all-start.2 = ((bf16[4,40,2560]{2,1,0:T(8,128)(2,1)}), bf16[4,40,2560]{2,1,0:T(8,128)(2,1)}, u32[]{:S(2)}, u32[]{:S(2)}) async-start(bf16[4,40,2560]{2,1,0:T(8,128)(2,1)} %bitcast.11), calls=%async_computation.2 | async-start | bytes 1638400 | tf_op jit(solution)/shard_map/all_to_all | solution.py:76
  160.3 3.7 %fusion.18 = f32[128,768]{1,0:T(8,128)S(1)} fusion(bf16[1,768,2560]{2,1,0:T(8,128)(2,1)} %all-gather.4.cloned.1.call-done, bf16[128,2560]{1,0:T(8,128)(2,1)S(1)} %copy-done.8, f32[128]{0:T(128)S(1)} %get-tuple-element.3), kind=kOutput, calls=%fused_computation.19 | convolution fusion | flops 504299520 | bytes 4981248 | tf_op jit(solution)/shard_map/dot_general | solution.py:8
  164.0 1.4 fusion.4
  166.2 1.4 fusion.23
  167.6 4.6 %all-to-all-done.2 = bf16[4,40,2560]{2,1,0:T(8,128)(2,1)} async-done(((bf16[4,40,2560]{2,1,0:T(8,128)(2,1)}), bf16[4,40,2560]{2,1,0:T(8,128)(2,1)}, u32[]{:S(2)}, u32[]{:S(2)}) %all-to-all-start.2) | async-done | bytes 819232 | tf_op jit(solution)/shard_map/all_to_all | solution.py:76
  172.2 2.4 %fusion.29 = bf16[128,2560]{1,0:T(8,128)(2,1)} fusion(f32[128,2560]{1,0:T(8,128)S(1)} %fusion.23, bf16[160,2560]{1,0:T(8,128)(2,1)} %bitcast.12, s32[128]{0:T(128)S(1)} %multiply_add_fusion), kind=kOutput, calls=%fused_computation.27 | convolution fusion | flops 105533440 | bytes 2785792 | tf_op jit(solution)/shard_map/dot_general | solution.py:90
  174.6 22.3 %reduce-scatter.2.cloned.1.call-done = bf16[96,2560]{1,0:T(8,128)(2,1)} async-done(((bf16[768,2560]{1,0:T(8,128)(2,1)}), bf16[96,2560]{1,0:T(8,128)(2,1)}) %reduce-scatter.2.cloned.1.call-update) | async-done | bytes 491536 | tf_op jit(solution)/shard_map/reduce_scatter | solution.py:96
  (41 shorter events, 5.9 us)
Async XLA Ops:
  7.2 4.7 %copy-start = (bf16[128,2560]{1,0:T(8,128)(2,1)S(1)}, bf16[128,2560]{1,0:T(8,128)(2,1)}, u32[]{:S(2)}) copy-start(bf16[128,2560]{1,0:T(8,128)(2,1)} %param.8) | copy-start | bytes 1966084
  7.2 11.7 %copy-start.12 = (s32[128,2]{0,1:T(2,128)S(1)}, s32[128,2]{0,1:T(2,128)}, u32[]{:S(2)}) copy-start(s32[128,2]{0,1:T(2,128)} %param.11) | copy-start | bytes 3076
  7.2 11.8 %copy-start.6 = (bf16[128,2560]{1,0:T(8,128)(2,1)S(1)}, bf16[128,2560]{1,0:T(8,128)(2,1)}, u32[]{:S(2)}) copy-start(bf16[128,2560]{1,0:T(8,128)(2,1)} %param.9) | copy-start | bytes 1966084
  7.2 50.0 %all-gather.8.cloned.1.call-start = ((), (), s32[]{:S(2)}) async-start(), calls=%async_computation.6 | async-start | bytes 4423680 | tf_op jit(solution)/shard_map/all_gather | solution.py:43
  7.9 94.5 %all-gather.6.cloned.1.call-start = ((), (), s32[]{:S(2)}) async-start(), calls=%async_computation.5 | async-start | bytes 4423680 | tf_op jit(solution)/shard_map/all_gather | solution.py:44
  8.7 139.1 %all-gather.4.cloned.1.call-start = ((), (), s32[]{:S(2)}) async-start(), calls=%async_computation.4 | async-start | bytes 4423680 | tf_op jit(solution)/shard_map/all_gather | solution.py:45
  13.1 46.9 %all-to-all-start.1 = ((bf16[4,40,2560]{2,1,0:T(8,128)(2,1)}), bf16[4,40,2560]{2,1,0:T(8,128)(2,1)S(1)}, u32[]{:S(2)}, u32[]{:S(2)}) async-start(bf16[4,40,2560]{2,1,0:T(8,128)(2,1)} %bitcast.9), calls=%async_computation.1 | async-start | bytes 1638400 | tf_op jit(solution)/shard_map/all_to_all | solution.py:70
  60.0 52.2 %all-to-all-start = ((bf16[4,40,2560]{2,1,0:T(8,128)(2,1)}), bf16[4,40,2560]{2,1,0:T(8,128)(2,1)S(1)}, u32[]{:S(2)}, u32[]{:S(2)}) async-start(bf16[4,40,2560]{2,1,0:T(8,128)(2,1)} %bitcast.56), calls=%async_computation | async-start | bytes 1638400 | tf_op jit(solution)/shard_map/all_to_all | solution.py:71
  63.6 133.2 %reduce-scatter.2.cloned.1.call-start = ((), (), s32[]{:S(2)}) async-start(), calls=%async_computation.7 | async-start | bytes 4423680 | tf_op jit(solution)/shard_map/reduce_scatter | solution.py:96
  102.5 3.9 %copy-start.1 = (bf16[1,2560,768]{2,1,0:T(8,128)(2,1)S(1)}, bf16[1,2560,768]{2,1,0:T(8,128)(2,1)}, u32[]{:S(2)}) copy-start(bf16[1,2560,768]{2,1,0:T(8,128)(2,1)} %all-gather.6.cloned.1.call-done) | copy-start | bytes 11796484
  102.5 5.3 %copy-start.7 = (bf16[128,2560]{1,0:T(8,128)(2,1)S(1)}, bf16[128,2560]{1,0:T(8,128)(2,1)}, u32[]{:S(2)}) copy-start(bf16[128,2560]{1,0:T(8,128)(2,1)} %param.9) | copy-start | bytes 1966084
  107.0 0.7 copy-start.10
  107.7 4.5 %copy-start.9 = (f32[160,768]{1,0:T(8,128)S(1)}, f32[160,768]{1,0:T(8,128)}, u32[]{:S(2)}) copy-start(f32[160,768]{1,0:T(8,128)} %fusion.10) | copy-start | bytes 1474564
  147.7 3.7 %copy-start.4 = (bf16[1,2560,768]{2,1,0:T(8,128)(2,1)S(1)}, bf16[1,2560,768]{2,1,0:T(8,128)(2,1)}, u32[]{:S(2)}) copy-start(bf16[1,2560,768]{2,1,0:T(8,128)(2,1)} %all-gather.8.cloned.1.call-done) | copy-start | bytes 11796484
  151.4 2.1 %copy-start.2 = (bf16[1,2560,768]{2,1,0:T(8,128)(2,1)S(1)}, bf16[1,2560,768]{2,1,0:T(8,128)(2,1)}, u32[]{:S(2)}) copy-start(bf16[1,2560,768]{2,1,0:T(8,128)(2,1)} %all-gather.6.cloned.1.call-done) | copy-start | bytes 11796484
  153.6 6.7 %copy-start.8 = (bf16[128,2560]{1,0:T(8,128)(2,1)S(1)}, bf16[128,2560]{1,0:T(8,128)(2,1)}, u32[]{:S(2)}) copy-start(bf16[128,2560]{1,0:T(8,128)(2,1)} %param.9) | copy-start | bytes 1966084
  155.9 8.1 %copy-start.11 = (f32[128,768]{1,0:T(8,128)S(1)}, f32[128,768]{1,0:T(8,128)}, u32[]{:S(2)}) copy-start(f32[128,768]{1,0:T(8,128)} %copy-done.10) | copy-start | bytes 1179652
  155.9 16.3 %all-to-all-start.2 = ((bf16[4,40,2560]{2,1,0:T(8,128)(2,1)}), bf16[4,40,2560]{2,1,0:T(8,128)(2,1)}, u32[]{:S(2)}, u32[]{:S(2)}) async-start(bf16[4,40,2560]{2,1,0:T(8,128)(2,1)} %bitcast.11), calls=%async_computation.2 | async-start | bytes 1638400 | tf_op jit(solution)/shard_map/all_to_all | solution.py:76
  160.3 3.7 %copy-start.5 = (bf16[1,2560,768]{2,1,0:T(8,128)(2,1)S(1)}, bf16[1,2560,768]{2,1,0:T(8,128)(2,1)}, u32[]{:S(2)}) copy-start(bf16[1,2560,768]{2,1,0:T(8,128)(2,1)} %all-gather.8.cloned.1.call-done) | copy-start | bytes 11796484
  164.0 2.2 %copy-start.3 = (bf16[1,2560,768]{2,1,0:T(8,128)(2,1)S(1)}, bf16[1,2560,768]{2,1,0:T(8,128)(2,1)}, u32[]{:S(2)}) copy-start(bf16[1,2560,768]{2,1,0:T(8,128)(2,1)} %all-gather.6.cloned.1.call-done) | copy-start | bytes 11796484
Sparse Core Ops, SparseCore 0:
  9.7 47.4 all-gather.7
  58.8 43.5 all-gather.5
  104.1 43.5 all-gather.3
  150.5 46.3 reduce-scatter.1
where the time goes:
time: 204 us; the launch traced here: 203 us
  waiting for transfers between devices  131 us (64%)
  matrix products  40.3 us (20%)
  between operations  14.6 us (7%)
  starting transfers between devices  13.3 us (7%)
  other arithmetic  2.41 us (1%)
  local copies, waits for them, and re-layouts  2.21 us (1%)
    all_gather x1, waiting for transfers between devices, local(): lax.all_gather(w_gate, 'replica', axis=1, tiled=True)  36.9 us
    all_gather x1, waiting for transfers between devices, local(): lax.all_gather(w_up, 'replica', axis=1, tiled=True)  35.6 us
    all_gather x1, waiting for transfers between devices, local(): lax.all_gather(w_down, 'replica', axis=1, tiled=True)  29.1 us
    reduce_scatter x1, waiting for transfers between devices, local(): lax.psum_scatter((lax.dot_general(hidden_home, q_home, contract, preferre...  22.3 us
    dot_general x6, matrix products, against_rows(): lax.dot_general(left, matrix, (((1,), (1,)), ((), ())), preferred_element...  14 us
    dot_general x1, matrix products, local(): lax.dot_general(flat_hidden, flat_q, contract, preferred_element_type=jnp...  6.42 us
    dot_general x2, matrix products, expert_backward(): gate_act = jnp.dot(inputs, gate_w, preferred_element_type=jnp.float32)  5.95 us
    all_to_all x1, starting transfers between devices, local(): lax.all_to_all(send_x, 'expert', split_axis=0, concat_axis=0, tiled=True)  5.16 us
  transfers between devices with their start and end apart: 7, of which 5 were waited for; matrix products, arithmetic and copies ran while one was open for 21% of the time, Pallas kernels for 0%

commit v1 on v0

v1 whole, which is shorter than its diff:
```python
import functools

import jax
import jax.numpy as jnp
from jax import lax
from jax.experimental import pallas as pl
from jax.experimental.pallas import tpu as pltpu
from jax.sharding import PartitionSpec as P

BF16 = jnp.bfloat16
F32 = jnp.float32
MESH = pl.DeviceIdType.MESH
TILE = 256


def dot(left, right):
    return jnp.dot(left, right, preferred_element_type=F32)


def dot_rows(left, right):
    return lax.dot_general(
        left, right, (((1,), (1,)), ((), ())), preferred_element_type=F32
    )


def each(start, stop, body):
    def step(i, carry):
        body(i)
        return carry

    lax.fori_loop(start, stop, step, 0)


def kernel(
    experts, stages, cores, cap,
    tok_ref, cot_ref, partner_ref, combine_ref, counts_ref, wg_ref, wu_ref, wd_ref,
    grad_ref, down_ref,
    wg, wu, wd, x_all, q_all, send_x, send_q, gate_act, up_act, hid, hid_t,
    gate_grad, up_grad, home, back_send, back_recv, place_t,
    own_sum, pair_send, pair_recv, sum_send, sum_recv,
    w_local, w_send, w_recv, w_pair_send, w_pair_recv,
    row_send, row_recv, row_local, back_send_sem, back_recv_sem, back_local,
    pair_send_sem, pair_recv_sem, sum_send_sem, sum_recv_sem,
):
    rows = tok_ref.shape[0]
    width = tok_ref.shape[1]
    away = experts * cap
    total = rows + away
    padded = hid.shape[0]
    units = wd.shape[0]
    shard = wd_ref.shape[1]
    me_e = lax.axis_index("expert")
    me_r = lax.axis_index("replica")
    z = me_r // cores
    core = me_r % cores
    sources = (wg_ref, wu_ref, wd_ref)
    stores = (wg, wu, wd)

    def at_stage(stage):
        return (me_e, stage * cores + core)

    sibling = (me_e, z * cores + (cores - 1 - core))

    barrier = pltpu.get_barrier_semaphore()

    def greet(device):
        pl.semaphore_signal(barrier, inc=1, device_id=device, device_id_type=MESH)

    @pl.when(z > 0)
    def _():
        greet(at_stage(z - 1))

    @pl.when(z < stages - 1)
    def _():
        greet(at_stage(z + 1))

    if cores == 2:
        greet(sibling)

    each(1, experts, lambda i: greet(((me_e + i) % experts, me_r)))
    ends = jnp.where(z > 0, 1, 0) + jnp.where(z < stages - 1, 1, 0)
    pl.semaphore_wait(barrier, ends + (cores - 1) + (experts - 1))

    def part(kind, stage, owner_core):
        length = sources[kind].shape[1]
        begin = pl.multiple_of((stage * cores + owner_core) * length, 16)
        return stores[kind].at[pl.ds(begin, length)]

    def along(kind, stage, way, own=False):
        return pltpu.make_async_remote_copy(
            src_ref=sources[kind].at[0] if own else part(kind, stage, core),
            dst_ref=part(kind, stage, core),
            send_sem=w_send.at[kind, stage, way],
            recv_sem=w_recv.at[kind, stage],
            device_id=at_stage(z - 1 if way == 0 else z + 1),
            device_id_type=MESH,
        )

    def across(kind, stage, own=False, owner=None):
        owner = core if owner is None else owner
        return pltpu.make_async_remote_copy(
            src_ref=sources[kind].at[0] if own else part(kind, stage, owner),
            dst_ref=part(kind, stage, owner),
            send_sem=w_pair_send.at[kind, stage],
            recv_sem=w_pair_recv.at[kind, stage],
            device_id=sibling,
            device_id_type=MESH,
        )

    def local_weight(kind):
        return pltpu.make_async_copy(
            sources[kind].at[0], part(kind, z, core), w_local.at[kind]
        )

    def start_down(k):
        @pl.when((z > 0) & (stages - 1 - z == k))
        def _():
            along(2, z, 0, True).start()

        @pl.when((z < stages - 1) & (z == k))
        def _():
            along(2, z, 1, True).start()

    for kind in (0, 1):
        @pl.when(z > 0)
        def _():
            along(kind, z, 0, True).start()

        @pl.when(z < stages - 1)
        def _():
            along(kind, z, 1, True).start()

    start_down(0)
    for kind in range(3):
        if cores == 2:
            across(kind, z, True).start()
        local_weight(kind).start()

    def pass_on(kind, k):
        @pl.when(z - k >= 0)
        def _():
            along(kind, z - k, 1).wait_recv()

            @pl.when(z < stages - 1)
            def _():
                along(kind, z - k, 1).start()

            if cores == 2:
                across(kind, z - k).start()

        @pl.when(z + k < stages)
        def _():
            along(kind, z + k, 0).wait_recv()

            @pl.when(z > 0)
            def _():
                along(kind, z + k, 0).start()

            if cores == 2:
                across(kind, z + k).start()

    ratios = combine_ref[...].astype(F32)
    ratio_sum = ratios[:, 0:1] + ratios[:, 1:2]
    real = lax.broadcasted_iota(jnp.int32, (rows, 1), 0) < counts_ref[...]
    share_home = jnp.where(real, ratios[:, 0:1] / ratio_sum, 0.0)
    share_away = jnp.where(real, ratios[:, 1:2] / ratio_sum, 0.0)
    lanes = 128
    partner = partner_ref[...]
    chosen = partner == lax.broadcasted_iota(jnp.int32, (rows, lanes), 1)
    chosen = jnp.where(chosen, 1.0, 0.0)
    earlier = lax.broadcasted_iota(jnp.int32, (rows, rows), 0) > lax.broadcasted_iota(
        jnp.int32, (rows, rows), 1
    )
    earlier = jnp.where(earlier, 1.0, 0.0).astype(BF16)
    rank = jnp.sum(dot(earlier, chosen.astype(BF16)) * chosen, axis=1, keepdims=True)
    slot = partner.astype(F32) * cap + rank
    slot_row = jnp.transpose(jnp.broadcast_to(slot, (rows, lanes)))[0:1, :]
    place_t[...] = jnp.where(
        slot == lax.broadcasted_iota(jnp.int32, (rows, away), 1).astype(F32), 1.0, 0.0
    ).astype(BF16)
    place = jnp.where(
        slot_row == lax.broadcasted_iota(jnp.int32, (away, rows), 0).astype(F32), 1.0, 0.0
    ).astype(BF16)

    def prepare(i):
        cols = pl.ds(pl.multiple_of(i * TILE, TILE), TILE)
        x = tok_ref[:, cols]
        upstream = cot_ref[:, cols].astype(F32)
        x_all[0:rows, cols] = x
        q_all[0:rows, cols] = (upstream * share_home).astype(BF16)
        send_x[:, cols] = dot(place, x).astype(BF16)
        send_q[:, cols] = dot(place, (upstream * share_away).astype(BF16)).astype(BF16)
        if padded > total:
            q_all[total:padded, cols] = jnp.zeros((padded - total, TILE), BF16)

    each(0, width // TILE, prepare)

    def slots(index, base=0):
        return pl.ds(pl.multiple_of(base + index * cap, 16), cap)

    def row_copy(which, other, block):
        return pltpu.make_async_remote_copy(
            src_ref=(send_x, send_q)[which].at[slots(other)],
            dst_ref=(x_all, q_all)[which].at[slots(block, rows)],
            send_sem=row_send.at[which, other],
            recv_sem=row_recv.at[which, block],
            device_id=(other, me_r),
            device_id_type=MESH,
        )

    def row_copy_local(which):
        return pltpu.make_async_copy(
            (send_x, send_q)[which].at[slots(me_e)],
            (x_all, q_all)[which].at[slots(me_e, rows)],
            row_local.at[which],
        )

    for which in (0, 1):
        each(1, experts, lambda i: row_copy(which, (me_e + i) % experts, me_e).start())
        row_copy_local(which).start()

    def first_weights(k):
        pass_on(0, k)
        pass_on(1, k)
        start_down(k)

    each(1, stages, first_weights)

    for which in (0, 1):
        def arrive(i):
            other = (me_e + i) % experts
            row_copy(which, other, other).wait_recv()

        each(1, experts, arrive)
        row_copy_local(which).wait()
    for kind in (0, 1):
        local_weight(kind).wait()
        if cores == 2:
            each(0, stages, lambda s: across(kind, s, owner=1 - core).wait_recv())

    if padded > total:
        hid[total:padded, :] = jnp.zeros((padded - total, TILE), F32)

    def forward(i):
        cols = pl.ds(pl.multiple_of(i * TILE, TILE), TILE)
        x = x_all[...]
        gate = dot(x, wg[:, cols])
        up = dot(x, wu[:, cols])
        gate_act[:, cols] = gate
        up_act[:, cols] = up
        hid[0:total, :] = gate * jax.nn.sigmoid(gate) * up
        hid_t[cols, :] = jnp.transpose(hid[...]).astype(BF16)

    each(0, units // TILE, forward)

    def partial(stage, owner_core):
        begin = pl.multiple_of((stage * cores + owner_core) * shard, 16)
        return dot(hid_t[pl.ds(begin, shard), :], q_all[...])

    def pair_copy(stage):
        return pltpu.make_async_remote_copy(
            src_ref=pair_send.at[stage],
            dst_ref=pair_recv.at[stage],
            send_sem=pair_send_sem.at[stage],
            recv_sem=pair_recv_sem.at[stage],
            device_id=sibling,
            device_id_type=MESH,
        )

    if cores == 2:
        def for_sibling(stage):
            pair_send[stage] = partial(stage, 1 - core).astype(BF16)
            pair_copy(stage).start()

        each(0, stages, for_sibling)

    def for_own(stage):
        mine = partial(stage, core)
        if cores == 2:
            pair_copy(stage).wait_recv()
            mine = mine + pair_recv[stage].astype(F32)
        own_sum[stage] = mine

    each(0, stages, for_own)

    def sum_copy(target, way):
        there = z - 1 if way == 0 else z + 1
        slot_there = target if way == 0 else jnp.where(target == there, stages, target)
        return pltpu.make_async_remote_copy(
            src_ref=sum_send.at[target],
            dst_ref=sum_recv.at[slot_there],
            send_sem=sum_send_sem.at[target],
            recv_sem=sum_recv_sem.at[slot_there],
            device_id=at_stage(there),
            device_id_type=MESH,
        )

    def sum_arrived(slot_here):
        pltpu.make_async_remote_copy(
            src_ref=sum_send.at[0],
            dst_ref=sum_recv.at[slot_here],
            send_sem=sum_send_sem.at[0],
            recv_sem=sum_recv_sem.at[slot_here],
            device_id=at_stage(jnp.where(z > 0, z - 1, z + 1)),
            device_id_type=MESH,
        ).wait_recv()

    def chain(j, at_end):
        low, high = j, stages - 1 - j

        @pl.when((low < z) & ((z == stages - 1) == at_end))
        def _():
            value = own_sum[low]
            if not at_end:
                sum_arrived(low)
                value = value + sum_recv[low].astype(F32)
            sum_send[low] = value.astype(BF16)
            sum_copy(low, 0).start()

        @pl.when((high > z) & ((z == 0) == at_end))
        def _():
            value = own_sum[high]
            if not at_end:
                sum_arrived(high)
                value = value + sum_recv[high].astype(F32)
            sum_send[high] = value.astype(BF16)
            sum_copy(high, 1).start()

    each(0, stages, lambda j: chain(j, True))

    each(1, stages, lambda k: pass_on(2, k))
    local_weight(2).wait()
    if cores == 2:
        each(0, stages, lambda s: across(2, s, owner=1 - core).wait_recv())

    def backward(i):
        cols = pl.ds(pl.multiple_of(i * TILE, TILE), TILE)
        hidden_grad = dot_rows(q_all[0:total, :], wd[cols, :])
        gate = gate_act[:, cols]
        s = jax.nn.sigmoid(gate)
        gate_grad[:, cols] = (
            hidden_grad * up_act[:, cols] * s * (1.0 + gate * (1.0 - s))
        ).astype(BF16)
        up_grad[:, cols] = (hidden_grad * (gate * s)).astype(BF16)

    each(0, units // TILE, backward)

    def inputs(i):
        cols = pl.ds(pl.multiple_of(i * TILE, TILE), TILE)
        value = dot_rows(gate_grad[...], wg[cols, :]) + dot_rows(up_grad[...], wu[cols, :])
        home[:, cols] = value[0:rows]
        back_send[:, cols] = value[rows:total].astype(BF16)

    each(0, width // TILE, inputs)

    def back_copy(other, block):
        return pltpu.make_async_remote_copy(
            src_ref=back_send.at[slots(other)],
            dst_ref=back_recv.at[slots(block)],
            send_sem=back_send_sem.at[other],
            recv_sem=back_recv_sem.at[block],
            device_id=(other, me_r),
            device_id_type=MESH,
        )

    def back_copy_local():
        return pltpu.make_async_copy(
            back_send.at[slots(me_e)], back_recv.at[slots(me_e)], back_local
        )

    each(1, experts, lambda i: back_copy((me_e + i) % experts, me_e).start())
    back_copy_local().start()

    each(0, stages, lambda j: chain(j, False))

    def back_arrive(i):
        other = (me_e + i) % experts
        back_copy(other, other).wait_recv()

    each(1, experts, back_arrive)
    back_copy_local().wait()

    def finish(i):
        cols = pl.ds(pl.multiple_of(i * TILE, TILE), TILE)
        grad_ref[:, cols] = (
            home[:, cols] + dot(place_t[...], back_recv[:, cols])
        ).astype(BF16)

    each(0, width // TILE, finish)

    @pl.when(z < stages - 1)
    def _():
        sum_arrived(z)
        own_sum[z] = own_sum[z] + sum_recv[z].astype(F32)

    @pl.when(z > 0)
    def _():
        sum_arrived(stages)
        own_sum[z] = own_sum[z] + sum_recv[stages].astype(F32)

    down_ref[0] = own_sum[z].astype(BF16)

    for kind in range(3):
        def sent(stage):
            @pl.when((stage >= z) & (z > 0))
            def _():
                along(kind, stage, 0).wait_send()

            @pl.when((stage <= z) & (z < stages - 1))
            def _():
                along(kind, stage, 1).wait_send()

            if cores == 2:
                across(kind, stage).wait_send()

        each(0, stages, sent)
    for which in (0, 1):
        each(1, experts, lambda i: row_copy(which, (me_e + i) % experts, me_e).wait_send())
    each(1, experts, lambda i: back_copy((me_e + i) % experts, me_e).wait_send())

    def sums_sent(stage):
        if cores == 2:
            pair_copy(stage).wait_send()

        @pl.when(stage < z)
        def _():
            sum_copy(stage, 0).wait_send()

        @pl.when(stage > z)
        def _():
            sum_copy(stage, 1).wait_send()

    each(0, stages, sums_sent)


def local(cores, tokens, cotangent, partner, combine, counts, w_gate, w_up, w_down):
    rows, width = tokens.shape
    experts = lax.axis_size("expert")
    replicas = lax.axis_size("replica")
    stages = replicas // cores
    slots = max(2, (5 * rows // 4 + experts - 1) // experts)
    cap = -(-slots // 16) * 16
    away = experts * cap
    total = rows + away
    padded = -(-total // 128) * 128
    units = w_gate.shape[2]
    shard = w_down.shape[1]
    dma = pltpu.SemaphoreType.DMA
    pairs = stages if cores == 2 else 1
    in_vmem = pl.BlockSpec(memory_space=pltpu.VMEM)
    in_place = pl.BlockSpec(memory_space=pl.ANY)
    return pl.pallas_call(
        functools.partial(kernel, experts, stages, cores, cap),
        out_shape=(
            jax.ShapeDtypeStruct((rows, width), BF16),
            jax.ShapeDtypeStruct((1, shard, width), BF16),
        ),
        in_specs=[in_vmem] * 5 + [in_place] * 3,
        out_specs=(in_vmem, in_vmem),
        scratch_shapes=[
            pltpu.VMEM((width, units), BF16),
            pltpu.VMEM((width, units), BF16),
            pltpu.VMEM((units, width), BF16),
            pltpu.VMEM((total, width), BF16),
            pltpu.VMEM((padded, width), BF16),
            pltpu.VMEM((away, width), BF16),
            pltpu.VMEM((away, width), BF16),
            pltpu.VMEM((total, units), F32),
            pltpu.VMEM((total, units), F32),
            pltpu.VMEM((padded, TILE), F32),
            pltpu.VMEM((units, padded), BF16),
            pltpu.VMEM((total, units), BF16),
            pltpu.VMEM((total, units), BF16),
            pltpu.VMEM((rows, width), F32),
            pltpu.VMEM((away, width), BF16),
            pltpu.VMEM((away, width), BF16),
            pltpu.VMEM((rows, away), BF16),
            pltpu.VMEM((stages, shard, width), F32),
            pltpu.VMEM((pairs, shard, width), BF16),
            pltpu.VMEM((pairs, shard, width), BF16),
            pltpu.VMEM((stages, shard, width), BF16),
            pltpu.VMEM((stages + 1, shard, width), BF16),
            dma((3,)),
            dma((3, stages, 2)),
            dma((3, stages)),
            dma((3, stages)),
            dma((3, stages)),
            dma((2, experts)),
            dma((2, experts)),
            dma((2,)),
            dma((experts,)),
            dma((experts,)),
            dma,
            dma((stages,)),
            dma((stages,)),
            dma((stages,)),
            dma((stages + 1,)),
        ],
        compiler_params=pltpu.CompilerParams(
            collective_id=0,
            has_side_effects=True,
            vmem_limit_bytes=60 * 2**20,
        ),
        cost_estimate=pl.CostEstimate(
            flops=12 * total * width * units,
            bytes_accessed=8 * rows * width + 6 * units * width,
            transcendentals=2 * total * units,
        ),
        name="expert_backward",
    )(tokens, cotangent, partner, combine, counts.reshape(1, 1), w_gate, w_up, w_down)


def cores_together(mesh):
    replicas = mesh.shape["replica"]
    if replicas % 2:
        return 1
    line = list(mesh.devices.reshape(-1)[:2])
    places = [getattr(device, "coords", None) for device in line]
    if None in places:
        return 2
    return 2 if tuple(places[0]) == tuple(places[1]) else 1


def solution(mesh):
    placed = (
        P(("expert", "replica"), None),
        P(("expert", "replica"), None),
        P(("expert", "replica"), None),
        P(("expert", "replica"), None),
        P(("expert", "replica")),
        P("expert", "replica", None),
        P("expert", "replica", None),
        P("expert", "replica", None),
    )
    return jax.shard_map(
        functools.partial(local, cores_together(mesh)),
        mesh=mesh,
        in_specs=placed,
        out_specs=(P(("expert", "replica"), None), P("expert", "replica", None)),
        check_vma=False,
    )
```

time: 204 us -> 135 us (0.66)
  the two profiles are of different devices: /device:TPU:0 before, /device:TPU:16 now
where the time goes in v1:
time: 135 us; the launch traced here: 134 us
  Pallas kernels  128 us (95%)
  local copies, waits for them, and re-layouts  4.94 us (4%)
    pallas_call x1, Pallas kernels, local(): pl.pallas_call(functools.partial(kernel, experts, stages, cores, cap), ou...  128 us
    unnamed x10, local copies, waits for them, and re-layouts  4.94 us

profile of v1, /device:TPU:16, one launch (start us, length us, event | category | flops | bytes accessed | tf_op | source)
XLA Modules:
  0.0 133.9 jit_solution(6904812591567568583)
XLA Ops:
  1.3 0.0 copy-start.2
  1.3 0.6 copy-done.2
  1.9 0.0 copy-start.1
  1.9 0.7 copy.10.partner_ref
  2.7 0.0 copy-done.1
  2.7 0.7 copy.11.combine_ref
  3.4 127.7 %expert_backward.1 = (bf16[128,2560]{1,0:T(8,128)(2,1)}, bf16[1,96,2560]{2,1,0:T(8,128)(2,1)}) custom-call(bf16[128,2560]{1,0:T(8,128)(2,1)} %tok_ref.1, bf16[128,2560]{1,0:T(8,128)(2,1)} %cot_ref.1, s32[128,1]{1,0:T(8,128)} %copy.10.partner_ref, s32[128,2]{1,0:T(8,128)} %copy.11.combine_ref, s32[1,1]{1,0:T(1,128)} %bitcast.1.counts_ref, ...), custom_call_target="tpu_custom_call" | custom-call | flops 7549747200 | bytes 14417920 | tf_op jit(solution)/shard_map/expert_backward/pallas_call | solution.py:452
  131.1 0.0 copy-start
  131.1 2.0 %copy.15 = bf16[128,2560]{1,0:T(8,128)(2,1)} copy(bf16[128,2560]{1,0:T(8,128)(2,1)} %get-tuple-element.4) | data formatting | bytes 1310720
  133.2 0.0 copy-done
  133.2 0.8 copy.16
Async XLA Ops:
  1.3 0.7 copy-start.2
  1.9 0.7 copy-start.1
  131.1 2.0 %copy-start = (bf16[1,96,2560]{2,1,0:T(8,128)(2,1)S(1)}, bf16[1,96,2560]{2,1,0:T(8,128)(2,1)}, u32[]{:S(2)}) copy-start(bf16[1,96,2560]{2,1,0:T(8,128)(2,1)} %get-tuple-element.5) | copy-start | bytes 1474564

commit v2 on v1

--- a/solution.py
+++ b/solution.py
@@ -32,15 +32,17 @@
 
 
 def kernel(
-    experts, stages, cores, cap,
+    experts, stages, cores, cap, hosting,
     tok_ref, cot_ref, partner_ref, combine_ref, counts_ref, wg_ref, wu_ref, wd_ref,
     grad_ref, down_ref,
     wg, wu, wd, x_all, q_all, send_x, send_q, gate_act, up_act, hid, hid_t,
     gate_grad, up_grad, home, back_send, back_recv, place_t,
-    own_sum, pair_send, pair_recv, sum_send, sum_recv,
+    own_sum, pair_sum, pair_send, pair_recv, sum_send, sum_recv,
+    guest_q, guest_hid_t, guest_grad, hosted_grad,
     w_local, w_send, w_recv, w_pair_send, w_pair_recv,
     row_send, row_recv, row_local, back_send_sem, back_recv_sem, back_local,
     pair_send_sem, pair_recv_sem, sum_send_sem, sum_recv_sem,
+    guest_send, guest_recv, hosted_send, hosted_recv,
 ):
     rows = tok_ref.shape[0]
     width = tok_ref.shape[1]
@@ -60,6 +62,17 @@
         return (me_e, stage * cores + core)
 
     sibling = (me_e, z * cores + (cores - 1 - core))
+    first, last = (1, stages - 2) if hosting else (0, stages - 1)
+    inner = (z >= first) & (z <= last)
+    outer = (z < first) | (z > last)
+    beside = jnp.where(z == 0, 1, jnp.where(z == stages - 1, stages - 2,
+                       jnp.where(z == 1, 0, stages - 1)))
+
+    def to_left(kind):
+        return z > (first if kind == 2 else 0)
+
+    def to_right(kind):
+        return z < (last if kind == 2 else stages - 1)
 
     barrier = pltpu.get_barrier_semaphore()
 
@@ -113,11 +126,11 @@
         )
 
     def start_down(k):
-        @pl.when((z > 0) & (stages - 1 - z == k))
+        @pl.when(to_left(2) & (stages - 1 - z == k))
         def _():
             along(2, z, 0, True).start()
 
-        @pl.when((z < stages - 1) & (z == k))
+        @pl.when(to_right(2) & (z == k))
         def _():
             along(2, z, 1, True).start()
 
@@ -133,47 +146,57 @@
     start_down(0)
     for kind in range(3):
         if cores == 2:
-            across(kind, z, True).start()
+            @pl.when(inner | (kind < 2))
+            def _():
+                across(kind, z, True).start()
+
         local_weight(kind).start()
 
     def pass_on(kind, k):
-        @pl.when(z - k >= 0)
+        takes = inner | (kind < 2)
+
+        @pl.when((z - k >= 0) & takes)
         def _():
             along(kind, z - k, 1).wait_recv()
 
-            @pl.when(z < stages - 1)
+            @pl.when(to_right(kind))
             def _():
                 along(kind, z - k, 1).start()
 
             if cores == 2:
                 across(kind, z - k).start()
 
-        @pl.when(z + k < stages)
+        @pl.when((z + k < stages) & takes)
         def _():
             along(kind, z + k, 0).wait_recv()
 
-            @pl.when(z > 0)
+            @pl.when(to_left(kind))
             def _():
                 along(kind, z + k, 0).start()
 
             if cores == 2:
                 across(kind, z + k).start()
 
+    lanes = 128
+
+    def column(row):
+        return jnp.transpose(jnp.broadcast_to(row, (lanes, rows)))[:, 0:1]
+
     ratios = combine_ref[...].astype(F32)
-    ratio_sum = ratios[:, 0:1] + ratios[:, 1:2]
+    ratio_home, ratio_away = column(ratios[0:1, :]), column(ratios[1:2, :])
+    ratio_sum = ratio_home + ratio_away
     real = lax.broadcasted_iota(jnp.int32, (rows, 1), 0) < counts_ref[...]
-    share_home = jnp.where(real, ratios[:, 0:1] / ratio_sum, 0.0)
-    share_away = jnp.where(real, ratios[:, 1:2] / ratio_sum, 0.0)
-    lanes = 128
-    partner = partner_ref[...]
-    chosen = partner == lax.broadcasted_iota(jnp.int32, (rows, lanes), 1)
+    share_home = jnp.where(real, ratio_home / ratio_sum, 0.0)
+    share_away = jnp.where(real, ratio_away / ratio_sum, 0.0)
+    partner = column(partner_ref[...].astype(F32))
+    chosen = partner == lax.broadcasted_iota(jnp.int32, (rows, lanes), 1).astype(F32)
     chosen = jnp.where(chosen, 1.0, 0.0)
     earlier = lax.broadcasted_iota(jnp.int32, (rows, rows), 0) > lax.broadcasted_iota(
         jnp.int32, (rows, rows), 1
     )
     earlier = jnp.where(earlier, 1.0, 0.0).astype(BF16)
     rank = jnp.sum(dot(earlier, chosen.astype(BF16)) * chosen, axis=1, keepdims=True)
-    slot = partner.astype(F32) * cap + rank
+    slot = partner * cap + rank
     slot_row = jnp.transpose(jnp.broadcast_to(slot, (rows, lanes)))[0:1, :]
     place_t[...] = jnp.where(
         slot == lax.broadcasted_iota(jnp.int32, (rows, away), 1).astype(F32), 1.0, 0.0
@@ -192,6 +215,8 @@
         send_q[:, cols] = dot(place, (upstream * share_away).astype(BF16)).astype(BF16)
         if padded > total:
             q_all[total:padded, cols] = jnp.zeros((padded - total, TILE), BF16)
+            if hosting:
+                guest_q[total:padded, cols] = jnp.zeros((padded - total, TILE), BF16)
 
     each(0, width // TILE, prepare)
 
@@ -219,6 +244,50 @@
         each(1, experts, lambda i: row_copy(which, (me_e + i) % experts, me_e).start())
         row_copy_local(which).start()
 
+    def guest_copy(index):
+        if index == 2:
+            source, target = hid_t, guest_hid_t
+        else:
+            span = slice(0, rows) if index == 0 else slice(rows, total)
+            source, target = q_all.at[span], guest_q.at[span]
+        return pltpu.make_async_remote_copy(
+            src_ref=source,
+            dst_ref=target,
+            send_sem=guest_send.at[index],
+            recv_sem=guest_recv.at[index],
+            device_id=at_stage(beside),
+            device_id_type=MESH,
+        )
+
+    def hosted_copy():
+        return pltpu.make_async_remote_copy(
+            src_ref=guest_grad,
+            dst_ref=hosted_grad,
+            send_sem=hosted_send,
+            recv_sem=hosted_recv,
+            device_id=at_stage(beside),
+            device_id_type=MESH,
+        )
+
+    def rows_arrive():
+        for which in (1, 0):
+            def arrive(i):
+                other = (me_e + i) % experts
+                row_copy(which, other, other).wait_recv()
+
+            each(1, experts, arrive)
+            row_copy_local(which).wait()
+            if hosting and which == 1:
+                @pl.when(outer)
+                def _():
+                    guest_copy(1).start()
+
+    if hosting:
+        @pl.when(outer)
+        def _():
+            guest_copy(0).start()
+            rows_arrive()
+
     def first_weights(k):
         pass_on(0, k)
         pass_on(1, k)
@@ -226,13 +295,10 @@
 
     each(1, stages, first_weights)
 
-    for which in (0, 1):
-        def arrive(i):
-            other = (me_e + i) % experts
-            row_copy(which, other, other).wait_recv()
-
-        each(1, experts, arrive)
-        row_copy_local(which).wait()
+    if hosting:
+        pl.when(inner)(rows_arrive)
+    else:
+        rows_arrive()
     for kind in (0, 1):
         local_weight(kind).wait()
         if cores == 2:
@@ -252,10 +318,10 @@
         hid_t[cols, :] = jnp.transpose(hid[...]).astype(BF16)
 
     each(0, units // TILE, forward)
-
-    def partial(stage, owner_core):
-        begin = pl.multiple_of((stage * cores + owner_core) * shard, 16)
-        return dot(hid_t[pl.ds(begin, shard), :], q_all[...])
+    if hosting:
+        @pl.when(outer)
+        def _():
+            guest_copy(2).start()
 
     def pair_copy(stage):
         return pltpu.make_async_remote_copy(
@@ -267,21 +333,35 @@
             device_id_type=MESH,
         )
 
-    if cores == 2:
-        def for_sibling(stage):
-            pair_send[stage] = partial(stage, 1 - core).astype(BF16)
-            pair_copy(stage).start()
-
-        each(0, stages, for_sibling)
-
-    def for_own(stage):
-        mine = partial(stage, core)
+    def partials():
+        if hosting:
+            guest_copy(2).wait_recv()
+
+        def product(stage):
+            length = cores * shard
+            span = pl.ds(pl.multiple_of(stage * length, 16), length)
+
+            def columns(i):
+                cols = pl.ds(pl.multiple_of(i * 2 * TILE, TILE), 2 * TILE)
+                value = dot(hid_t[span, :], q_all[:, cols])
+                if hosting:
+                    value = value + dot(guest_hid_t[span, :], guest_q[:, cols])
+                for owner in range(cores):
+                    pair_sum[owner, :, cols] = value[owner * shard : (owner + 1) * shard]
+
+            each(0, width // (2 * TILE), columns)
+            own_sum[stage] = pair_sum[core]
+            if cores == 2:
+                pair_send[stage] = pair_sum[1 - core].astype(BF16)
+                pair_copy(stage).start()
+
+        each(0, stages, product)
         if cores == 2:
-            pair_copy(stage).wait_recv()
-            mine = mine + pair_recv[stage].astype(F32)
-        own_sum[stage] = mine
-
-    each(0, stages, for_own)
+            def joined(stage):
+                pair_copy(stage).wait_recv()
+                own_sum[stage] = own_sum[stage] + pair_recv[stage].astype(F32)
+
+            each(0, stages, joined)
 
     def sum_copy(target, way):
         there = z - 1 if way == 0 else z + 1
@@ -308,7 +388,7 @@
     def chain(j, at_end):
         low, high = j, stages - 1 - j
 
-        @pl.when((low < z) & ((z == stages - 1) == at_end))
+        @pl.when((low < z) & ((z == last) == at_end) & inner)
         def _():
             value = own_sum[low]
             if not at_end:
@@ -317,7 +397,7 @@
             sum_send[low] = value.astype(BF16)
             sum_copy(low, 0).start()
 
-        @pl.when((high > z) & ((z == 0) == at_end))
+        @pl.when((high > z) & ((z == first) == at_end) & inner)
         def _():
             value = own_sum[high]
             if not at_end:
@@ -326,16 +406,23 @@
             sum_send[high] = value.astype(BF16)
             sum_copy(high, 1).start()
 
-    each(0, stages, lambda j: chain(j, True))
+    if not hosting:
+        partials()
+        each(0, stages, lambda j: chain(j, True))
 
     each(1, stages, lambda k: pass_on(2, k))
     local_weight(2).wait()
     if cores == 2:
-        each(0, stages, lambda s: across(2, s, owner=1 - core).wait_recv())
-
-    def backward(i):
+        @pl.when(inner)
+        def _():
+            each(0, stages, lambda s: across(2, s, owner=1 - core).wait_recv())
+
+    def backward(i, hosted=False):
         cols = pl.ds(pl.multiple_of(i * TILE, TILE), TILE)
-        hidden_grad = dot_rows(q_all[0:total, :], wd[cols, :])
+        if hosted:
+            hidden_grad = hosted_grad[:, cols].astype(F32)
+        else:
+            hidden_grad = dot_rows(q_all[0:total, :], wd[cols, :])
         gate = gate_act[:, cols]
         s = jax.nn.sigmoid(gate)
         gate_grad[:, cols] = (
@@ -343,7 +430,25 @@
         ).astype(BF16)
         up_grad[:, cols] = (hidden_grad * (gate * s)).astype(BF16)
 
-    each(0, units // TILE, backward)
+    def for_guest(i):
+        cols = pl.ds(pl.multiple_of(i * TILE, TILE), TILE)
+        guest_grad[:, cols] = dot_rows(guest_q[0:total, :], wd[cols, :]).astype(BF16)
+
+    if hosting:
+        @pl.when(inner)
+        def _():
+            guest_copy(0).wait_recv()
+            guest_copy(1).wait_recv()
+            each(0, units // TILE, for_guest)
+            hosted_copy().start()
+            each(0, units // TILE, backward)
+
+        @pl.when(outer)
+        def _():
+            hosted_copy().wait_recv()
+            each(0, units // TILE, lambda i: backward(i, True))
+    else:
+        each(0, units // TILE, backward)
 
     def inputs(i):
         cols = pl.ds(pl.multiple_of(i * TILE, TILE), TILE)
@@ -351,34 +456,37 @@
         home[:, cols] = value[0:rows]
         back_send[:, cols] = value[rows:total].astype(BF16)
 
-    each(0, width // TILE, inputs)
-
-    def back_copy(other, block):
-        return pltpu.make_async_remote_copy(
-            src_ref=back_send.at[slots(other)],
-            dst_ref=back_recv.at[slots(block)],
-            send_sem=back_send_sem.at[other],
-            recv_sem=back_recv_sem.at[block],
+    half = width // 2
+
+    def back_copy(part, other, block):
+        cols = pl.ds(part * half, half)
+        return pltpu.make_async_remote_copy(
+            src_ref=back_send.at[slots(other), cols],
+            dst_ref=back_recv.at[slots(block), cols],
+            send_sem=back_send_sem.at[part, other],
+            recv_sem=back_recv_sem.at[part, block],
             device_id=(other, me_r),
             device_id_type=MESH,
         )
 
-    def back_copy_local():
+    def back_copy_local(part):
+        cols = pl.ds(part * half, half)
         return pltpu.make_async_copy(
-            back_send.at[slots(me_e)], back_recv.at[slots(me_e)], back_local
-        )
-
-    each(1, experts, lambda i: back_copy((me_e + i) % experts, me_e).start())
-    back_copy_local().start()
-
+            back_send.at[slots(me_e), cols],
+            back_recv.at[slots(me_e), cols],
+            back_local.at[part],
+        )
+
+    tiles = half // TILE
+    for part_ in (0, 1):
+        each(part_ * tiles, (part_ + 1) * tiles, inputs)
+        each(1, experts, lambda i: back_copy(part_, (me_e + i) % experts, me_e).start())
+        back_copy_local(part_).start()
+
+    if hosting:
+        pl.when(inner)(partials)
+        each(0, stages, lambda j: chain(j, True))
     each(0, stages, lambda j: chain(j, False))
-
-    def back_arrive(i):
-        other = (me_e + i) % experts
-        back_copy(other, other).wait_recv()
-
-    each(1, experts, back_arrive)
-    back_copy_local().wait()
 
     def finish(i):
         cols = pl.ds(pl.multiple_of(i * TILE, TILE), TILE)
@@ -386,14 +494,26 @@
             home[:, cols] + dot(place_t[...], back_recv[:, cols])
         ).astype(BF16)
 
-    each(0, width // TILE, finish)
-
-    @pl.when(z < stages - 1)
+    for part_ in (0, 1):
+        def back_arrive(i):
+            other = (me_e + i) % experts
+            back_copy(part_, other, other).wait_recv()
+
+        each(1, experts, back_arrive)
+        back_copy_local(part_).wait()
+        each(part_ * tiles, (part_ + 1) * tiles, finish)
+
+    if hosting:
+        @pl.when(outer)
+        def _():
+            own_sum[z] = jnp.zeros(own_sum.shape[1:], F32)
+
+    @pl.when(z < last)
     def _():
         sum_arrived(z)
         own_sum[z] = own_sum[z] + sum_recv[z].astype(F32)
 
-    @pl.when(z > 0)
+    @pl.when(z > first)
     def _():
         sum_arrived(stages)
         own_sum[z] = own_sum[z] + sum_recv[stages].astype(F32)
@@ -402,21 +522,23 @@
 
     for kind in range(3):
         def sent(stage):
-            @pl.when((stage >= z) & (z > 0))
+            @pl.when((stage >= z) & to_left(kind))
             def _():
                 along(kind, stage, 0).wait_send()
 
-            @pl.when((stage <= z) & (z < stages - 1))
+            @pl.when((stage <= z) & to_right(kind))
             def _():
                 along(kind, stage, 1).wait_send()
 
             if cores == 2:
-                across(kind, stage).wait_send()
+                @pl.when(inner | (kind < 2))
+                def _():
+                    across(kind, stage).wait_send()
 
         each(0, stages, sent)
     for which in (0, 1):
         each(1, experts, lambda i: row_copy(which, (me_e + i) % experts, me_e).wait_send())
-    each(1, experts, lambda i: back_copy((me_e + i) % experts, me_e).wait_send())
+        each(1, experts, lambda i: back_copy(which, (me_e + i) % experts, me_e).wait_send())
 
     def sums_sent(stage):
         if cores == 2:
@@ -430,7 +552,18 @@
         def _():
             sum_copy(stage, 1).wait_send()
 
-    each(0, stages, sums_sent)
+    if hosting:
+        @pl.when(inner)
+        def _():
+            each(0, stages, sums_sent)
+            hosted_copy().wait_send()
+
+        @pl.when(outer)
+        def _():
+            for index in range(3):
+                guest_copy(index).wait_send()
+    else:
+        each(0, stages, sums_sent)
 
 
 def local(cores, tokens, cotangent, partner, combine, counts, w_gate, w_up, w_down):
@@ -443,6 +576,7 @@
     away = experts * cap
     total = rows + away
     padded = -(-total // 128) * 128
+    hosting = stages == 4
     units = w_gate.shape[2]
     shard = w_down.shape[1]
     dma = pltpu.SemaphoreType.DMA
@@ -450,7 +584,7 @@
     in_vmem = pl.BlockSpec(memory_space=pltpu.VMEM)
     in_place = pl.BlockSpec(memory_space=pl.ANY)
     return pl.pallas_call(
-        functools.partial(kernel, experts, stages, cores, cap),
+        functools.partial(kernel, experts, stages, cores, cap, hosting),
         out_shape=(
             jax.ShapeDtypeStruct((rows, width), BF16),
             jax.ShapeDtypeStruct((1, shard, width), BF16),
@@ -476,10 +610,15 @@
             pltpu.VMEM((away, width), BF16),
             pltpu.VMEM((rows, away), BF16),
             pltpu.VMEM((stages, shard, width), F32),
+            pltpu.VMEM((cores, shard, width), F32),
             pltpu.VMEM((pairs, shard, width), BF16),
             pltpu.VMEM((pairs, shard, width), BF16),
             pltpu.VMEM((stages, shard, width), BF16),
             pltpu.VMEM((stages + 1, shard, width), BF16),
+            pltpu.VMEM((padded if hosting else 16, width), BF16),
+            pltpu.VMEM((units if hosting else 16, padded), BF16),
+            pltpu.VMEM((total if hosting else 16, units), BF16),
+            pltpu.VMEM((total if hosting else 16, units), BF16),
             dma((3,)),
             dma((3, stages, 2)),
             dma((3, stages)),
@@ -488,13 +627,17 @@
             dma((2, experts)),
             dma((2, experts)),
             dma((2,)),
-            dma((experts,)),
-            dma((experts,)),
-            dma,
+            dma((2, experts)),
+            dma((2, experts)),
+            dma((2,)),
             dma((stages,)),
             dma((stages,)),
             dma((stages,)),
             dma((stages + 1,)),
+            dma((3,)),
+            dma((3,)),
+            dma,
+            dma,
         ],
         compiler_params=pltpu.CompilerParams(
             collective_id=0,
@@ -507,7 +650,7 @@
             transcendentals=2 * total * units,
         ),
         name="expert_backward",
-    )(tokens, cotangent, partner, combine, counts.reshape(1, 1), w_gate, w_up, w_down)
+    )(tokens, cotangent, partner.T, combine.T, counts.reshape(1, 1), w_gate, w_up, w_down)
 
 
 def cores_together(mesh):

time: 135 us -> 130 us (0.963)
  the two profiles are of different devices: /device:TPU:16 before, /device:TPU:0 now
where the time goes in v2:
time: 130 us; the launch traced here: 129 us
  Pallas kernels  125 us (96%)
  local copies, waits for them, and re-layouts  2.8 us (2%)
    pallas_call x1, Pallas kernels, local(): pl.pallas_call(functools.partial(kernel, experts, stages, cores, cap, hos...  125 us
    unnamed x4, local copies, waits for them, and re-layouts  2.8 us

profile of v2, /device:TPU:0, one launch (start us, length us, event | category | flops | bytes accessed | tf_op | source)
XLA Modules:
  0.0 129.4 jit_solution(10135021324650249189)
XLA Ops:
  1.3 125.3 %expert_backward.1 = (bf16[128,2560]{1,0:T(8,128)(2,1)}, bf16[1,96,2560]{2,1,0:T(8,128)(2,1)}) custom-call(bf16[128,2560]{1,0:T(8,128)(2,1)} %tok_ref.1, bf16[128,2560]{1,0:T(8,128)(2,1)} %cot_ref.1, s32[1,128]{1,0:T(1,128)} %bitcast.5, s32[2,128]{1,0:T(2,128)} %bitcast.4, s32[1,1]{1,0:T(1,128)} %bitcast.3.counts_ref, bf16[1,320,768]{2,1,0:T(8,128)(2,1)} %wg_ref.1, ...), custom_call_target="tpu_custom_call" | custom-call | flops 7549747200 | bytes 14417920 | tf_op jit(solution)/shard_map/expert_backward/pallas_call | solution.py:586
  126.6 0.0 copy-start
  126.6 2.0 %copy.13 = bf16[128,2560]{1,0:T(8,128)(2,1)} copy(bf16[128,2560]{1,0:T(8,128)(2,1)} %get-tuple-element.4) | data formatting | bytes 1310720
  128.6 0.0 copy-done
  128.6 0.8 copy.14
Async XLA Ops:
  126.6 2.0 %copy-start = (bf16[1,96,2560]{2,1,0:T(8,128)(2,1)S(1)}, bf16[1,96,2560]{2,1,0:T(8,128)(2,1)}, u32[]{:S(2)}) copy-start(bf16[1,96,2560]{2,1,0:T(8,128)(2,1)} %get-tuple-element.5) | copy-start | bytes 1474564

commit v3 on v2

--- a/solution.py
+++ b/solution.py
@@ -55,8 +55,12 @@
     me_r = lax.axis_index("replica")
     z = me_r // cores
     core = me_r % cores
-    sources = (wg_ref, wu_ref, wd_ref)
-    stores = (wg, wu, wd)
+    tiles_h = units // TILE
+    tile_order = [0] + [tiles_h - 1] * (tiles_h > 1) + list(range(1, tiles_h - 1))
+    pieces = [(which, tile) for tile in tile_order for which in (0, 1)] + [(2, 0)]
+    down = len(pieces) - 1
+    early = min(4, down)
+    phases = (range(0, early), range(early, down), range(down, down + 1))
 
     def at_stage(stage):
         return (me_e, stage * cores + core)
@@ -69,10 +73,10 @@
                        jnp.where(z == 1, 0, stages - 1)))
 
     def to_left(kind):
-        return z > (first if kind == 2 else 0)
+        return z > (first if kind == down else 0)
 
     def to_right(kind):
-        return z < (last if kind == 2 else stages - 1)
+        return z < (last if kind == down else stages - 1)
 
     barrier = pltpu.get_barrier_semaphore()
 
@@ -95,13 +99,23 @@
     pl.semaphore_wait(barrier, ends + (cores - 1) + (experts - 1))
 
     def part(kind, stage, owner_core):
-        length = sources[kind].shape[1]
+        which, tile = pieces[kind]
+        length = (wg_ref, wu_ref, wd_ref)[which].shape[1]
         begin = pl.multiple_of((stage * cores + owner_core) * length, 16)
-        return stores[kind].at[pl.ds(begin, length)]
+        span = pl.ds(begin, length)
+        if kind == down:
+            return wd.at[span]
+        return (wg, wu)[which].at[span, pl.ds(tile * TILE, TILE)]
+
+    def mine(kind):
+        which, tile = pieces[kind]
+        if kind == down:
+            return wd_ref.at[0]
+        return (wg_ref, wu_ref)[which].at[0, :, pl.ds(tile * TILE, TILE)]
 
     def along(kind, stage, way, own=False):
         return pltpu.make_async_remote_copy(
-            src_ref=sources[kind].at[0] if own else part(kind, stage, core),
+            src_ref=mine(kind) if own else part(kind, stage, core),
             dst_ref=part(kind, stage, core),
             send_sem=w_send.at[kind, stage, way],
             recv_sem=w_recv.at[kind, stage],
@@ -112,7 +126,7 @@
     def across(kind, stage, own=False, owner=None):
         owner = core if owner is None else owner
         return pltpu.make_async_remote_copy(
-            src_ref=sources[kind].at[0] if own else part(kind, stage, owner),
+            src_ref=mine(kind) if own else part(kind, stage, owner),
             dst_ref=part(kind, stage, owner),
             send_sem=w_pair_send.at[kind, stage],
             recv_sem=w_pair_recv.at[kind, stage],
@@ -122,38 +136,40 @@
 
     def local_weight(kind):
         return pltpu.make_async_copy(
-            sources[kind].at[0], part(kind, z, core), w_local.at[kind]
-        )
-
-    def start_down(k):
-        @pl.when(to_left(2) & (stages - 1 - z == k))
-        def _():
-            along(2, z, 0, True).start()
-
-        @pl.when(to_right(2) & (z == k))
-        def _():
-            along(2, z, 1, True).start()
-
-    for kind in (0, 1):
-        @pl.when(z > 0)
+            mine(kind), part(kind, z, core), w_local.at[kind]
+        )
+
+    def start_own(phase, k):
+        for kind in phases[phase]:
+            @pl.when(to_left(kind) & (stages - 1 - z == k))
+            def _():
+                along(kind, z, 0, True).start()
+
+            @pl.when(to_right(kind) & (z == k))
+            def _():
+                along(kind, z, 1, True).start()
+
+    for kind in phases[0]:
+        @pl.when(to_left(kind))
         def _():
             along(kind, z, 0, True).start()
 
-        @pl.when(z < stages - 1)
+        @pl.when(to_right(kind))
         def _():
             along(kind, z, 1, True).start()
 
-    start_down(0)
-    for kind in range(3):
+    start_own(1, 0)
+    start_own(2, 0)
+    for kind in range(down + 1):
         if cores == 2:
-            @pl.when(inner | (kind < 2))
+            @pl.when(inner | (kind < down))
             def _():
                 across(kind, z, True).start()
 
         local_weight(kind).start()
 
     def pass_on(kind, k):
-        takes = inner | (kind < 2)
+        takes = inner | (kind < down)
 
         @pl.when((z - k >= 0) & takes)
         def _():
@@ -245,8 +261,9 @@
         row_copy_local(which).start()
 
     def guest_copy(index):
-        if index == 2:
-            source, target = hid_t, guest_hid_t
+        if index >= 2:
+            span = pl.ds(tile_order[index - 2] * TILE, TILE)
+            source, target = hid_t.at[span], guest_hid_t.at[span]
         else:
             span = slice(0, rows) if index == 0 else slice(rows, total)
             source, target = q_all.at[span], guest_q.at[span]
@@ -288,27 +305,31 @@
             guest_copy(0).start()
             rows_arrive()
 
-    def first_weights(k):
-        pass_on(0, k)
-        pass_on(1, k)
-        start_down(k)
-
-    each(1, stages, first_weights)
+    def travel(phase, k):
+        for kind in phases[phase]:
+            pass_on(kind, k)
+        if phase < 2:
+            start_own(phase + 1, k)
+
+    def landed(phase):
+        for kind in phases[phase]:
+            local_weight(kind).wait()
+            if cores == 2:
+                @pl.when(inner | (kind < down))
+                def _():
+                    each(0, stages, lambda s: across(kind, s, owner=1 - core).wait_recv())
+
+    each(1, stages, lambda k: travel(0, k))
 
     if hosting:
         pl.when(inner)(rows_arrive)
     else:
         rows_arrive()
-    for kind in (0, 1):
-        local_weight(kind).wait()
-        if cores == 2:
-            each(0, stages, lambda s: across(kind, s, owner=1 - core).wait_recv())
-
     if padded > total:
         hid[total:padded, :] = jnp.zeros((padded - total, TILE), F32)
 
-    def forward(i):
-        cols = pl.ds(pl.multiple_of(i * TILE, TILE), TILE)
+    def forward(tile):
+        cols = slice(tile * TILE, (tile + 1) * TILE)
         x = x_all[...]
         gate = dot(x, wg[:, cols])
         up = dot(x, wu[:, cols])
@@ -317,11 +338,15 @@
         hid[0:total, :] = gate * jax.nn.sigmoid(gate) * up
         hid_t[cols, :] = jnp.transpose(hid[...]).astype(BF16)
 
-    each(0, units // TILE, forward)
-    if hosting:
-        @pl.when(outer)
-        def _():
-            guest_copy(2).start()
+    for phase in (0, 1):
+        if phase == 1:
+            each(1, stages, lambda k: travel(1, k))
+        landed(phase)
+        for order, tile in enumerate(tile_order):
+            if 2 * order in phases[phase]:
+                forward(tile)
+                if hosting:
+                    pl.when(outer)(lambda: guest_copy(2 + order).start())
 
     def pair_copy(stage):
         return pltpu.make_async_remote_copy(
@@ -333,11 +358,9 @@
             device_id_type=MESH,
         )
 
-    def partials():
-        if hosting:
-            guest_copy(2).wait_recv()
-
-        def product(stage):
+    def partials(stage_of, count):
+        def product(i):
+            stage = stage_of(i)
             length = cores * shard
             span = pl.ds(pl.multiple_of(stage * length, 16), length)
 
@@ -355,13 +378,14 @@
                 pair_send[stage] = pair_sum[1 - core].astype(BF16)
                 pair_copy(stage).start()
 
-        each(0, stages, product)
+        each(0, count, product)
         if cores == 2:
-            def joined(stage):
+            def joined(i):
+                stage = stage_of(i)
                 pair_copy(stage).wait_recv()
                 own_sum[stage] = own_sum[stage] + pair_recv[stage].astype(F32)
 
-            each(0, stages, joined)
+            each(0, count, joined)
 
     def sum_copy(target, way):
         there = z - 1 if way == 0 else z + 1
@@ -406,16 +430,22 @@
             sum_send[high] = value.astype(BF16)
             sum_copy(high, 1).start()
 
-    if not hosting:
-        partials()
+    if hosting:
+        travel(2, 1)
+
+        @pl.when(inner)
+        def _():
+            for index in range(4):
+                guest_copy(index).wait_recv()
+            partials(lambda i: i * (stages - 1), 2)
+            chain(0, True)
+
+        each(2, stages, lambda k: travel(2, k))
+    else:
+        partials(lambda i: i, stages)
         each(0, stages, lambda j: chain(j, True))
-
-    each(1, stages, lambda k: pass_on(2, k))
-    local_weight(2).wait()
-    if cores == 2:
-        @pl.when(inner)
-        def _():
-            each(0, stages, lambda s: across(2, s, owner=1 - core).wait_recv())
+        each(1, stages, lambda k: travel(2, k))
+    landed(2)
 
     def backward(i, hosted=False):
         cols = pl.ds(pl.multiple_of(i * TILE, TILE), TILE)
@@ -437,10 +467,9 @@
     if hosting:
         @pl.when(inner)
         def _():
-            guest_copy(0).wait_recv()
-            guest_copy(1).wait_recv()
             each(0, units // TILE, for_guest)
             hosted_copy().start()
+            chain(0, False)
             each(0, units // TILE, backward)
 
         @pl.when(outer)
@@ -484,9 +513,14 @@
         back_copy_local(part_).start()
 
     if hosting:
-        pl.when(inner)(partials)
-        each(0, stages, lambda j: chain(j, True))
-    each(0, stages, lambda j: chain(j, False))
+        @pl.when(inner)
+        def _():
+            guest_copy(4).wait_recv()
+            partials(lambda i: i + 1, stages - 2)
+            chain(1, True)
+            chain(1, False)
+    else:
+        each(0, stages, lambda j: chain(j, False))
 
     def finish(i):
         cols = pl.ds(pl.multiple_of(i * TILE, TILE), TILE)
@@ -520,7 +554,7 @@
 
     down_ref[0] = own_sum[z].astype(BF16)
 
-    for kind in range(3):
+    for kind in range(down + 1):
         def sent(stage):
             @pl.when((stage >= z) & to_left(kind))
             def _():
@@ -531,7 +565,7 @@
                 along(kind, stage, 1).wait_send()
 
             if cores == 2:
-                @pl.when(inner | (kind < 2))
+                @pl.when(inner | (kind < down))
                 def _():
                     across(kind, stage).wait_send()
 
@@ -560,7 +594,7 @@
 
         @pl.when(outer)
         def _():
-            for index in range(3):
+            for index in range(5):
                 guest_copy(index).wait_send()
     else:
         each(0, stages, sums_sent)
@@ -576,8 +610,9 @@
     away = experts * cap
     total = rows + away
     padded = -(-total // 128) * 128
-    hosting = stages == 4
     units = w_gate.shape[2]
+    hosting = stages == 4 and units == 3 * TILE
+    pieces = 2 * (units // TILE) + 1
     shard = w_down.shape[1]
     dma = pltpu.SemaphoreType.DMA
     pairs = stages if cores == 2 else 1
@@ -619,11 +654,11 @@
             pltpu.VMEM((units if hosting else 16, padded), BF16),
             pltpu.VMEM((total if hosting else 16, units), BF16),
             pltpu.VMEM((total if hosting else 16, units), BF16),
-            dma((3,)),
-            dma((3, stages, 2)),
-            dma((3, stages)),
-            dma((3, stages)),
-            dma((3, stages)),
+            dma((pieces,)),
+            dma((pieces, stages, 2)),
+            dma((pieces, stages)),
+            dma((pieces, stages)),
+            dma((pieces, stages)),
             dma((2, experts)),
             dma((2, experts)),
             dma((2,)),
@@ -634,8 +669,8 @@
             dma((stages,)),
             dma((stages,)),
             dma((stages + 1,)),
-            dma((3,)),
-            dma((3,)),
+            dma((5,)),
+            dma((5,)),
             dma,
             dma,
         ],

time: 130 us -> 131 us (level)
  the two profiles are of different devices: /device:TPU:0 before, /device:TPU:16 now
where the time goes in v3:
time: 131 us
  Pallas kernels  127 us (97%)
  local copies, waits for them, and re-layouts  2.8 us (2%)
    pallas_call x1, Pallas kernels, local(): pl.pallas_call(functools.partial(kernel, experts, stages, cores, cap, hos...  127 us
    unnamed x4, local copies, waits for them, and re-layouts  2.8 us

profile of v3, /device:TPU:16, one launch (start us, length us, event | category | flops | bytes accessed | tf_op | source)
XLA Modules:
  0.0 130.9 jit_solution(66114368892110023)
XLA Ops:
  1.3 126.8 %expert_backward.1 = (bf16[128,2560]{1,0:T(8,128)(2,1)}, bf16[1,96,2560]{2,1,0:T(8,128)(2,1)}) custom-call(bf16[128,2560]{1,0:T(8,128)(2,1)} %tok_ref.1, bf16[128,2560]{1,0:T(8,128)(2,1)} %cot_ref.1, s32[1,128]{1,0:T(1,128)} %bitcast.5, s32[2,128]{1,0:T(2,128)} %bitcast.4, s32[1,1]{1,0:T(1,128)} %bitcast.3.counts_ref, bf16[1,320,768]{2,1,0:T(8,128)(2,1)} %wg_ref.1, ...), custom_call_target="tpu_custom_call" | custom-call | flops 7549747200 | bytes 14417920 | tf_op jit(solution)/shard_map/expert_backward/pallas_call | solution.py:621
  128.1 0.0 copy-start
  128.1 2.0 %copy.13 = bf16[128,2560]{1,0:T(8,128)(2,1)} copy(bf16[128,2560]{1,0:T(8,128)(2,1)} %get-tuple-element.4) | data formatting | bytes 1310720
  130.1 0.0 copy-done
  130.1 0.8 copy.14
Async XLA Ops:
  128.1 2.0 %copy-start = (bf16[1,96,2560]{2,1,0:T(8,128)(2,1)S(1)}, bf16[1,96,2560]{2,1,0:T(8,128)(2,1)}, u32[]{:S(2)}) copy-start(bf16[1,96,2560]{2,1,0:T(8,128)(2,1)} %get-tuple-element.5) | copy-start | bytes 1474564

commit v4 on v3

--- a/solution.py
+++ b/solution.py
@@ -276,12 +276,13 @@
             device_id_type=MESH,
         )
 
-    def hosted_copy():
+    def hosted_copy(tile):
+        cols = pl.ds(tile * TILE, TILE)
         return pltpu.make_async_remote_copy(
-            src_ref=guest_grad,
-            dst_ref=hosted_grad,
-            send_sem=hosted_send,
-            recv_sem=hosted_recv,
+            src_ref=guest_grad.at[:, cols],
+            dst_ref=hosted_grad.at[:, cols],
+            send_sem=hosted_send.at[tile],
+            recv_sem=hosted_recv.at[tile],
             device_id=at_stage(beside),
             device_id_type=MESH,
         )
@@ -431,16 +432,7 @@
             sum_copy(high, 1).start()
 
     if hosting:
-        travel(2, 1)
-
-        @pl.when(inner)
-        def _():
-            for index in range(4):
-                guest_copy(index).wait_recv()
-            partials(lambda i: i * (stages - 1), 2)
-            chain(0, True)
-
-        each(2, stages, lambda k: travel(2, k))
+        each(1, stages, lambda k: travel(2, k))
     else:
         partials(lambda i: i, stages)
         each(0, stages, lambda j: chain(j, True))
@@ -448,7 +440,7 @@
     landed(2)
 
     def backward(i, hosted=False):
-        cols = pl.ds(pl.multiple_of(i * TILE, TILE), TILE)
+        cols = pl.ds(i * TILE, TILE) if hosted else pl.ds(pl.multiple_of(i * TILE, TILE), TILE)
         if hosted:
             hidden_grad = hosted_grad[:, cols].astype(F32)
         else:
@@ -461,21 +453,28 @@
         up_grad[:, cols] = (hidden_grad * (gate * s)).astype(BF16)
 
     def for_guest(i):
-        cols = pl.ds(pl.multiple_of(i * TILE, TILE), TILE)
+        cols = pl.ds(i * TILE, TILE)
         guest_grad[:, cols] = dot_rows(guest_q[0:total, :], wd[cols, :]).astype(BF16)
 
     if hosting:
         @pl.when(inner)
         def _():
-            each(0, units // TILE, for_guest)
-            hosted_copy().start()
-            chain(0, False)
+            guest_copy(0).wait_recv()
+            guest_copy(1).wait_recv()
+            for tile in range(tiles_h):
+                for_guest(tile)
+                hosted_copy(tile).start()
+            guest_copy(2).wait_recv()
+            guest_copy(3).wait_recv()
+            partials(lambda i: i * (stages - 1), 2)
+            chain(0, True)
             each(0, units // TILE, backward)
 
         @pl.when(outer)
         def _():
-            hosted_copy().wait_recv()
-            each(0, units // TILE, lambda i: backward(i, True))
+            for tile in range(tiles_h):
+                hosted_copy(tile).wait_recv()
+                backward(tile, True)
     else:
         each(0, units // TILE, backward)
 
@@ -511,6 +510,10 @@
         each(part_ * tiles, (part_ + 1) * tiles, inputs)
         each(1, experts, lambda i: back_copy(part_, (me_e + i) % experts, me_e).start())
         back_copy_local(part_).start()
+        if hosting and part_ == 0:
+            @pl.when(inner)
+            def _():
+                chain(0, False)
 
     if hosting:
         @pl.when(inner)
@@ -590,7 +593,8 @@
         @pl.when(inner)
         def _():
             each(0, stages, sums_sent)
-            hosted_copy().wait_send()
+            for tile in range(tiles_h):
+                hosted_copy(tile).wait_send()
 
         @pl.when(outer)
         def _():
@@ -671,8 +675,8 @@
             dma((stages + 1,)),
             dma((5,)),
             dma((5,)),
-            dma,
-            dma,
+            dma((3,)),
+            dma((3,)),
         ],
         compiler_params=pltpu.CompilerParams(
             collective_id=0,

time: 131 us -> 127 us (0.969)
  Pallas kernels: 127 us -> 123 us
    pallas_call x1, Pallas kernels: 127 us -> 123 us  [local(): pl.pallas_call(functools.partial(kernel, experts, stages, cores, cap, hos...]
where the time goes in v4:
time: 127 us
  Pallas kernels  123 us (97%)
  local copies, waits for them, and re-layouts  2.8 us (2%)
  between operations  1.29 us (1%)
    pallas_call x1, Pallas kernels, local(): pl.pallas_call(functools.partial(kernel, experts, stages, cores, cap, hos...  123 us
    unnamed x4, local copies, waits for them, and re-layouts  2.8 us

profile of v4, /device:TPU:16, one launch (start us, length us, event | category | flops | bytes accessed | tf_op | source)
XLA Modules:
  0.0 126.7 jit_solution(3999771184049296646)
XLA Ops:
  1.3 122.6 %expert_backward.1 = (bf16[128,2560]{1,0:T(8,128)(2,1)}, bf16[1,96,2560]{2,1,0:T(8,128)(2,1)}) custom-call(bf16[128,2560]{1,0:T(8,128)(2,1)} %tok_ref.1, bf16[128,2560]{1,0:T(8,128)(2,1)} %cot_ref.1, s32[1,128]{1,0:T(1,128)} %bitcast.5, s32[2,128]{1,0:T(2,128)} %bitcast.4, s32[1,1]{1,0:T(1,128)} %bitcast.3.counts_ref, bf16[1,320,768]{2,1,0:T(8,128)(2,1)} %wg_ref.1, ...), custom_call_target="tpu_custom_call" | custom-call | flops 7549747200 | bytes 14417920 | tf_op jit(solution)/shard_map/expert_backward/pallas_call | solution.py:625
  123.8 0.0 copy-start
  123.9 2.0 %copy.13 = bf16[128,2560]{1,0:T(8,128)(2,1)} copy(bf16[128,2560]{1,0:T(8,128)(2,1)} %get-tuple-element.4) | data formatting | bytes 1310720
  125.9 0.0 copy-done
  125.9 0.8 copy.14
Async XLA Ops:
  123.8 2.0 %copy-start = (bf16[1,96,2560]{2,1,0:T(8,128)(2,1)S(1)}, bf16[1,96,2560]{2,1,0:T(8,128)(2,1)}, u32[]{:S(2)}) copy-start(bf16[1,96,2560]{2,1,0:T(8,128)(2,1)} %get-tuple-element.5) | copy-start | bytes 1474564
